TPU v7x, 128 devices: a whole 4x4x4 slice. The times are simulated.
128 devices in a mesh: dp: 32 (over z, y, core), seq: 4 (over x).
Axes of the slice: x: 4, y: 4, z: 4, core: 2. Of those that a mesh axis runs over, the one named last changes fastest.
Arguments:
- frames: bfloat16 [768, 64, 1536], P('seq', 'dp'), may hold values from -6 to 6
- lengths: int32 [64], P('dp'), may hold values from 96 to 768, as said below
- attn_gain: float32 [1536], replicated, may hold values from 0.5 to 1.5
- w_qkv: bfloat16 [3, 1536, 1536], P(None, 'dp', 'seq'), may hold values from -2 to 2
- w_out: bfloat16 [1536, 1536], P('seq', 'dp'), may hold values from -0.15625 to 0.15625
- conv_gain: float32 [1536], replicated, may hold values from 0.5 to 1.5
- w_pw1: bfloat16 [1536, 3072], P(('dp', 'seq')), may hold values from -0.15625 to 0.15625
- depth_kernel: float32 [31, 1536], replicated, may hold values from -1 to 1
- mid_gain: float32 [1536], replicated, may hold values from 0.5 to 1.5
- w_pw2: bfloat16 [1536, 1536], P(('dp', 'seq')), may hold values from -0.15625 to 0.15625
Outputs:
- layer_out: bfloat16 [768, 64, 1536], P('seq', 'dp')
Inputs may be any that keep to these rules, and one draw needn't show every extreme that they name: `lengths`: some utterance has exactly 768 valid frames.
All inputs are finite; a program needn't handle non-finite values.
Results may differ from a plain program's by a relative error of at most 0.018.
Values may be sent and summed in bfloat16 or wider, within the bound.
A program may use at most 128 MiB of HBM per device.

v0:
```python
import jax
import jax.numpy as jnp
from jax import lax
from jax.sharding import PartitionSpec as P

HD = 64
KERNEL = 31
HALO = 15


def padded_2(shard, sides, width):
    for axis, dim in sides:
        size, length = (lax.axis_size(axis), shard.shape[dim])
        up = [(i, (i + 1) % size) for i in range(size - 1)]
        down = [(j, i) for i, j in up]
        last = lax.slice_in_dim(shard, length - width, length, axis=dim)
        initial = lax.slice_in_dim(shard, 0, width, axis=dim)
        before = lax.ppermute(last, axis, up)
        after = lax.ppermute(initial, axis, down)
        shard = jnp.concatenate([before, shard, after], axis=dim)
    return shard


def layer_norm(values, gain):
    average = jnp.mean(values, -1, keepdims=True)
    centred = values - average
    spread = jnp.mean(centred * centred, -1, keepdims=True)
    return centred * lax.rsqrt(spread + 1e-05) * gain


def local(
    frames, lengths, attn_gain, w_qkv, w_out, conv_gain, w_pw1, depth_kernel, mid_gain, w_pw2
):
    local_len, utt_count, width = frames.shape
    total_len = local_len * lax.axis_size("seq")
    positions = lax.axis_index("seq") * local_len + lax.iota(jnp.int32, local_len)
    inside = positions[:, None] < lengths[None, :]
    normed = layer_norm(frames.astype(jnp.float32), attn_gain).astype(jnp.bfloat16)
    all_frames = lax.all_gather(normed, "seq", axis=0, tiled=True)
    qkv_cols, out_cols = (
        lax.all_gather(w_qkv, "dp", axis=1, tiled=True),
        lax.all_gather(w_out, "dp", axis=1, tiled=True),
    )
    qkv = jnp.einsum(
        "tud,cde->ctue", all_frames, qkv_cols, preferred_element_type=jnp.float32
    ).astype(jnp.bfloat16)
    head_share = qkv.shape[-1]
    heads_here = head_share // HD

    def to_items(matrix):
        shaped = matrix.reshape(total_len, utt_count, heads_here, HD).transpose(1, 2, 0, 3)
        return shaped.reshape(utt_count * heads_here, total_len, HD)

    key_block = total_len // 4
    score_scale = HD ** (-0.5)

    def attend(head_item):
        queries, key_rows, value_rows, length = head_item
        blocks_scores = []
        for block_index in range(4):
            first_key = block_index * key_block

            def scores_of(first_key=first_key):
                block_keys = key_rows[first_key : first_key + key_block]
                raw = (
                    jnp.einsum("qd,kd->qk", queries, block_keys, preferred_element_type=jnp.float32)
                    * score_scale
                )
                key_inside = first_key + lax.iota(jnp.int32, key_block) < length
                return jnp.where(key_inside[None, :], raw, -jnp.inf)

            blocks_scores.append(scores_of())
        weights = jax.nn.softmax(jnp.concatenate(blocks_scores, axis=-1), axis=-1).astype(
            jnp.bfloat16
        )
        running = jnp.zeros((total_len, HD), jnp.float32)
        for block_index in range(4):
            first_key = block_index * key_block

            def block_product(first_key=first_key):
                return jnp.dot(
                    weights[:, first_key : first_key + key_block],
                    value_rows[first_key : first_key + key_block],
                    preferred_element_type=jnp.float32,
                )

            running = running + block_product()
        return running.astype(jnp.bfloat16)

    item_lengths = jnp.repeat(lengths, heads_here)
    context_items = lax.map(
        attend, (to_items(qkv[0]), to_items(qkv[1]), to_items(qkv[2]), item_lengths)
    )
    context = context_items.reshape(utt_count, heads_here, total_len, HD).transpose(2, 0, 1, 3)
    context = context.reshape(total_len, utt_count, head_share)
    frame_rows = lax.slice_in_dim(context, 0, local_len * lax.axis_size("seq"), axis=0)
    attended = lax.psum_scatter(
        jnp.einsum("tue,ef->tuf", frame_rows, out_cols, preferred_element_type=jnp.float32).astype(
            jnp.bfloat16
        ),
        "seq",
        scatter_dimension=0,
        tiled=True,
    ).astype(jnp.float32)
    residual = (frames.astype(jnp.float32) + attended).astype(jnp.bfloat16)
    conv_in = layer_norm(residual.astype(jnp.float32), conv_gain).astype(jnp.bfloat16)
    weight_piece = lax.all_gather(w_pw1, ("dp", "seq"), axis=0, tiled=True)
    input_cols = lax.slice_in_dim(conv_in, 0, weight_piece.shape[0], axis=2)
    projection = jnp.zeros((local_len, utt_count, 2 * width), jnp.float32) + jnp.einsum(
        "tud,de->tue", input_cols, weight_piece, preferred_element_type=jnp.float32
    )
    gated = projection[..., :width] * jax.nn.sigmoid(projection[..., width:])
    gated = jnp.where(inside[..., None], gated, 0.0).astype(jnp.bfloat16)
    padded = padded_2(gated, (("seq", 0),), HALO)
    widened = padded.astype(jnp.float32)
    depthwise = jnp.zeros((local_len, utt_count, width), jnp.float32)
    for kernel_tap in range(KERNEL):
        depthwise = (
            depthwise + widened[kernel_tap : kernel_tap + local_len] * depth_kernel[kernel_tap]
        )
    hidden = layer_norm(depthwise, mid_gain)
    activated = (hidden * jax.nn.sigmoid(hidden)).astype(jnp.bfloat16)
    weight_piece = lax.all_gather(w_pw2, ("dp", "seq"), axis=0, tiled=True)
    input_cols = lax.slice_in_dim(activated, 0, weight_piece.shape[0], axis=2)
    projected = jnp.zeros((local_len, utt_count, width), jnp.float32) + jnp.einsum(
        "tud,de->tue", input_cols, weight_piece, preferred_element_type=jnp.float32
    )
    result = jnp.where(inside[..., None], residual.astype(jnp.float32) + projected, 0.0)
    return result.astype(jnp.bfloat16)


def solution(mesh):
    in_specs = (
        P("seq", "dp", None),
        P("dp"),
        P(),
        P(None, "dp", "seq"),
        P("seq", "dp"),
        P(),
        P(("dp", "seq"), None),
        P(),
        P(),
        P(("dp", "seq"), None),
    )
    out_specs = P("seq", "dp", None)
    return jax.shard_map(local, mesh=mesh, in_specs=in_specs, out_specs=out_specs, check_vma=False)
```

profile of v0, /device:TPU:1, one launch (start us, length us, event | category | flops | bytes accessed | tf_op | source)
XLA Modules:
  0.0 490.3 jit_solution(2614299149650716500)
XLA Ops:
  9.6 1.7 fusion.46
  13.8 46.0 %all-gather.10.cloned.1.call-done = bf16[3,1536,384]{2,1,0:T(8,128)(2,1)} async-done(((bf16[3,48,384]{2,1,0:T(8,128)(2,1)}), bf16[3,1536,384]{2,1,0:T(8,128)(2,1)}) %all-gather.10.cloned.1.call-update) | async-done | bytes 3538960 | tf_op jit(solution)/shard_map/all_gather | solution.py:41
  59.8 53.1 %all-gather.8.cloned.1.call-done = bf16[768,2,1536]{2,0,1:T(8,128)(2,1)} async-done(((bf16[192,2,1536]{2,0,1:T(8,128)(2,1)}), bf16[768,2,1536]{2,0,1:T(8,128)(2,1)}) %all-gather.8.cloned.1.call-update) | async-done | bytes 4718608 | tf_op jit(solution)/shard_map/all_gather | solution.py:39
  112.9 8.7 %convert_bitcast_fusion = bf16[3,768,2,384]{1,3,0,2:T(8,128)(2,1)S(1)} fusion(bf16[3,1536,384]{2,1,0:T(8,128)(2,1)} %all-gather.10.cloned.1.call-done, bf16[768,2,1536]{2,0,1:T(8,128)(2,1)} %all-gather.8.cloned.1.call-done), kind=kOutput, calls=%fused_computation.56 | convolution fusion | flops 5437587456 | bytes 11796480 | tf_op jit(solution)/shard_map/tud,cde->ctue/dot_general | solution.py:44
  122.8 3.7 copy.24
  126.5 2.4 copy.25
  128.9 2.4 copy.26
  131.4 146.9 %while.10 = (s32[]{:T(128)}, bf16[12,768,64]{1,2,0:T(8,128)(2,1)}, s32[12]{0:T(128)S(1)}, bf16[12,768,64]{2,1,0:T(8,128)(2,1)}, bf16[12,768,64]{2,1,0:T(8,128)(2...) while((s32[]{:T(128)}, bf16[12,768,64]{1,2,0:T(8,128)(2,1)}, ...), condition=%wide.region_8.9_spmd, body=%wide.region_2.8_spmd.sunk | while | flops 159448896 | bytes 11943101 | solution.py:91
  141.9 1.7 fusion.130
  154.3 1.7 fusion.130
  166.5 1.7 fusion.130
  178.7 1.7 fusion.130
  191.0 1.7 fusion.130
  203.2 1.7 fusion.130
  215.4 1.7 fusion.130
  227.6 1.7 fusion.130
  239.9 1.7 fusion.130
  252.1 1.7 fusion.130
  264.3 1.7 fusion.130
  276.5 1.7 fusion.130
  278.2 6.4 %convolution_convert_fusion = bf16[768,2,1536]{2,0,1:T(8,128)(2,1)} fusion(bf16[768,2,384]{0,2,1:T(8,128)(2,1)} %bitcast.131, bf16[384,1536]{0,1:T(8,128)(2,1)} %all-gather.12.cloned.1.call-done), kind=kOutput, calls=%fused_computation.54 | convolution fusion | flops 1814298624 | bytes 7077888 | tf_op jit(solution)/shard_map/tue,ef->tuf/dot_general | solution.py:98
  286.2 50.9 %reduce-scatter.2.cloned.1.call-done = bf16[192,2,1536]{2,0,1:T(8,128)(2,1)} async-done(((bf16[768,2,1536]{2,0,1:T(8,128)(2,1)}), bf16[192,2,1536]{2,0,1:T(8,128)(2,1)}) %reduce-scatter.2.cloned.1.call-update) | async-done | bytes 1179664 | tf_op jit(solution)/shard_map/reduce_scatter | solution.py:97
  337.1 1.6 convert_reduce_fusion
  339.2 48.5 %all-gather.14.cloned.1.call-done = bf16[128,12,3072]{2,1,0:T(8,128)(2,1)} async-done(((bf16[1,12,3072]{2,1,0:T(8,128)(2,1)}), bf16[128,12,3072]{2,1,0:T(8,128)(2,1)}) %all-gather.14.cloned.1.call-update) | async-done | bytes 9437200 | tf_op jit(solution)/shard_map/all_gather | solution.py:107
  387.7 13.7 %reshape.170 = bf16[1536,3072,1]{1,0,2:T(8,128)(2,1)} reshape(bf16[128,12,3072]{2,1,0:T(8,128)(2,1)} %all-gather.14.cloned.1.call-done) | data formatting | bytes 18874368
  401.4 6.5 %fusion.86 = f32[192,2,3072]{2,0,1:T(8,128)S(1)} fusion(bf16[1536,3072,1]{1,0,2:T(8,128)(2,1)} %reshape.170, bf16[192,2,1536]{2,0,1:T(8,128)(2,1)S(1)} %get-tuple-element.84, f32[1536]{0:T(1024)S(1)} %copy-done.4, f32[192,2]{0,1:T(2,128)S(1)} %add_rsqrt_fusion.1, f32[192,2]{0,1:T(2,128)S(1)} %broadcast_multiply_fusion.1), kind=kOutput, calls=%fused_computation.147 | convolution fusion | flops 3626827776 | bytes 15344640 | tf_op jit(solution)/shard_map/tud,de->tue/dot_general | solution.py:109
  408.5 2.9 collective-permute-start
  413.0 45.4 %all-gather.16.cloned.1.call-done = bf16[128,12,1536]{2,1,0:T(8,128)(2,1)} async-done(((bf16[1,12,1536]{2,1,0:T(8,128)(2,1)}), bf16[128,12,1536]{2,1,0:T(8,128)(2,1)}) %all-gather.16.cloned.1.call-update) | async-done | bytes 4718608 | tf_op jit(solution)/shard_map/all_gather | solution.py:123
  458.4 8.2 %reshape.171 = bf16[1536,1536,1]{1,0,2:T(8,128)(2,1)} reshape(bf16[128,12,1536]{2,1,0:T(8,128)(2,1)} %all-gather.16.cloned.1.call-done) | data formatting | bytes 9437184
  467.0 11.0 %fusion.97 = (f32[192,2]{0,1:T(2,128)S(1)}, f32[192,2,1536]{2,0,1:T(8,128)S(1)}) fusion(f32[1536]{0:T(1024)S(1)} %get-tuple-element.67, f32[222,2,1536]{2,0,1:T(8,128)S(1)} %maximum_convert_fusion, f32[1536]{0:T(1024)S(1)} %get-tuple-element.68, f32[1536]{0:T(1024)S(1)} %get-tuple-element.39, f32[1536]{0:T(1024)S(1)} %get-tuple-element.40, ...), kind=kLoop, calls=%fused_computation.196 | loop fusion | flops 36568704 | bytes 75689472 | tf_op jit(solution)/shard_map/reduce_sum | solution.py:25
  478.7 2.2 fusion.38
  480.9 2.2 copy.28
  (210 shorter events, 137.5 us)
Async XLA Ops:
  7.4 4.0 copy-start
  7.4 4.0 copy-start.2
  7.4 52.5 %all-gather.10.cloned.1.call-start = ((), (), s32[]{:S(2)}) async-start(), calls=%async_computation.2 | async-start | bytes 3649536 | tf_op jit(solution)/shard_map/all_gather | solution.py:41
  8.1 104.8 %all-gather.8.cloned.1.call-start = ((), (), s32[]{:S(2)}) async-start(), calls=%async_computation.1 | async-start | bytes 5898240 | tf_op jit(solution)/shard_map/all_gather | solution.py:39
  9.6 4.0 copy-start.3
  12.8 265.4 %all-gather.12.cloned.1.call-start = ((), (), s32[]{:S(2)}) async-start(), calls=%async_computation.3 | async-start | bytes 1216512 | tf_op jit(solution)/shard_map/all_gather | solution.py:42
  13.6 323.5 %reduce-scatter.2.cloned.1.call-start = ((), (), s32[]{:S(2)}) async-start(), calls=%async_computation.4 | async-start | bytes 5898240 | tf_op jit(solution)/shard_map/reduce_scatter | solution.py:97
  284.6 1.2 copy-start.1
  284.7 103.0 %all-gather.14.cloned.1.call-start = ((), (), s32[]{:S(2)}) async-start(), calls=%async_computation.5 | async-start | bytes 12681216 | tf_op jit(solution)/shard_map/all_gather | solution.py:107
  285.2 173.1 %all-gather.16.cloned.1.call-start = ((), (), s32[]{:S(2)}) async-start(), calls=%async_computation.6 | async-start | bytes 6340608 | tf_op jit(solution)/shard_map/all_gather | solution.py:123
  339.2 62.2 %copy-start.4 = (f32[1536]{0:T(1024)S(1)}, f32[1536]{0:T(1024)}, u32[]{:S(2)}) copy-start(f32[1536]{0:T(1024)} %param.17) | copy-start | bytes 18436
  408.5 58.0 %collective-permute-start = (bf16[15,2,1536]{2,0,1:T(8,128)(2,1)S(1)}, bf16[15,2,1536]{2,0,1:T(8,128)(2,1)S(1)}, u32[]{:S(2)}, u32[]{:S(2)}) collective-permute-start(bf16[15,2,1536]{2,0,1:T(8,128)(2,1)S(1)} %get-tuple-element.100), channel_id=1, source_target_pairs={{0,1},{1,2},{2,3},{4,5},{5,6},{6,7},{8,9},{9,10},{10,11},{12,13},{... | collective-permute-start | bytes 276488 | tf_op jit(solution)/shard_map/ppermute | solution.py:18
  411.4 55.1 %collective-permute-start.1 = (bf16[15,2,1536]{2,0,1:T(8,128)(2,1)S(1)}, bf16[15,2,1536]{2,0,1:T(8,128)(2,1)S(1)}, u32[]{:S(2)}, u32[]{:S(2)}) collective-permute-start(bf16[15,2,1536]{2,0,1:T(8,128)(2,1)S(1)} %get-tuple-element.101), channel_id=1, source_target_pairs={{1,0},{2,1},{3,2},{5,4},{6,5},{7,6},{9,8},{10,9},{11,10},{13,12},{... | collective-permute-start | bytes 276488 | tf_op jit(solution)/shard_map/ppermute | solution.py:19
  467.0 11.5 %slice-start = ((s8[4718592]{0:T(1024)(128)(4,1)}), s8[4194304]{0:T(1024)(128)(4,1)S(1)}, s32[]{:S(2)}) async-start(s8[4718592]{0:T(1024)(128)(4,1)} %bitcast.127), calls=%async_computation.7 | async-start | bytes 8388608
  467.0 11.5 %slice-start.1 = ((s8[4718592]{0:T(1024)(128)(4,1)}), s8[524288]{0:T(1024)(128)(4,1)S(1)}, s32[]{:S(2)}) async-start(s8[4718592]{0:T(1024)(128)(4,1)} %bitcast.127), calls=%async_computation.8 | async-start | bytes 1048576
  478.0 0.7 copy-start.5
Sparse Core Ops, SparseCore 0:
  10.6 49.2 all-gather.9
  61.5 51.3 all-gather.7
  115.2 44.0 all-gather.11
  284.8 52.2 reduce-scatter.1
Sparse Core Ops, SparseCore 1:
  288.1 99.5 all-gather.13
  390.6 67.8 all-gather.15
where the time goes:
time: 495 us; the launch traced here: 490 us
  waiting for transfers between devices  246 us (50%)
  matrix products  139 us (28%)
  other arithmetic  43.6 us (9%)
  local copies, waits for them, and re-layouts  42.2 us (9%)
  between operations  14.8 us (3%)
    dot_general x48, matrix products, scores_of(): jnp.einsum('qd,kd->qk', queries, block_keys, preferred_element_type=jnp.f...  57.7 us
    dot_general x48, matrix products, block_product(): jnp.dot(weights[:, first_key:first_key + key_block], value_rows[first_key...  57.1 us
    all_gather x1, waiting for transfers between devices, local(): all_frames = lax.all_gather(normed, 'seq', axis=0, tiled=True)  53.1 us
    reduce_scatter x1, waiting for transfers between devices, local(): lax.psum_scatter(jnp.einsum('tue,ef->tuf', frame_rows, out_cols, preferre...  50.9 us
    all_gather x1, waiting for transfers between devices, local(): weight_piece = lax.all_gather(w_pw1, ('dp', 'seq'), axis=0, tiled=True)  48.5 us
    all_gather x1, waiting for transfers between devices, local(): lax.all_gather(w_qkv, 'dp', axis=1, tiled=True)  46 us
    all_gather x1, waiting for transfers between devices, local(): weight_piece = lax.all_gather(w_pw2, ('dp', 'seq'), axis=0, tiled=True)  45.4 us
    unnamed x18, local copies, waits for them, and re-layouts  22.2 us
  transfers between devices with their start and end apart: 8, of which 5 were waited for; matrix products, arithmetic and copies ran while one was open for 41% of the time, Pallas kernels for 0%

commit v1 on v0

v1 whole, which is shorter than its diff:
```python
import functools

import jax
import jax.numpy as jnp
from jax import lax
from jax.experimental import pallas as pl
from jax.experimental.pallas import tpu as pltpu
from jax.sharding import PartitionSpec as P

HD = 64
KERNEL = 31
D = 1536
T = 768
L = 192
EDGE = 16
BF = jnp.bfloat16
F32 = jnp.float32
SCALE = 1.4426950408889634 / 8.0
NSEM = 96
ROWS = 32


def sigmoid(v):
    return 0.5 * jnp.tanh(0.5 * v) + 0.5


def norm_rows(v, gain):
    mean = jnp.mean(v, -1, keepdims=True)
    centred = v - mean
    spread = jnp.mean(centred * centred, -1, keepdims=True)
    return centred * lax.rsqrt(spread + 1e-05) * gain


def chunks(buf, lanes, first=0, count=32, mat=None):
    out = []
    for i in range(first, first + count):
        z, y, c = i // 8, (i // 2) % 4, i % 2
        where = (c, z, y) if c == 0 else (c, y, z)
        if mat is not None:
            where = where + (mat,)
        out.append(buf[where + (slice(None), lanes)])
    return jnp.concatenate(out, axis=0)


def body(
    lens, frames, gain_a, w_qkv, w_out, gain_c, w_pw, taps, gain_m, out,
    bq, bo, b1, b2, xg, nrm, nsend, qkv, kbias, ctxl, ctx, res, cin, gp, cf, dep, send, recv,
):
    x = lax.axis_index("seq")
    dp = lax.axis_index("dp")
    z, y, c = lax.div(dp, 8), lax.rem(lax.div(dp, 2), 4), lax.rem(dp, 2)
    a, b = lax.div(x, 2), lax.rem(x, 2)

    def mod4(v):
        return lax.rem(v, 4)

    A = (1 - c) * y + c * z
    B = (1 - c) * z + c * y

    def dev(Bv, Av):
        return (1 - c) * (Bv * 8 + Av * 2) + c * (Av * 8 + Bv * 2 + 1)

    Ap, Am, Bp, Bm, Bf = mod4(A + 1), mod4(A + 3), mod4(B + 1), mod4(B + 3), mod4(B + 2)
    dAp, dAm, dBp, dBm = dev(B, Ap), dev(B, Am), dev(Bp, A), dev(Bm, A)
    sib = dp + 1 - 2 * c
    near, mate, far = 3 - x, x + 1 - 2 * b, mod4(x + 2)

    names = {}

    def rc(name, src, dst, to_dp, to_x):
        i = names.setdefault(name, len(names))
        return pltpu.make_async_remote_copy(
            src_ref=src, dst_ref=dst, send_sem=send.at[i], recv_sem=recv.at[i],
            device_id=(to_dp, to_x), device_id_type=pl.DeviceIdType.MESH,
        )

    barrier = pltpu.get_barrier_semaphore()
    peers = [(dp, mod4(x + d)) for d in (1, 2, 3)]
    peers += [(d, x) for d in (dAp, dAm, dBp, dBm, sib)]
    for peer in peers:
        pl.semaphore_signal(barrier, inc=1, device_id=peer, device_id_type=pl.DeviceIdType.MESH)

    class Ring:
        def __init__(self, key, buf, half):
            same = lambda n, ref, to: rc(key + n, ref, ref, to, x)
            lo, hi = pl.ds(0, half), pl.ds(half, half)
            mid = (slice(None),) * (len(buf.shape) - 4)
            self.p1 = [same("p1+", buf.at[c, B, A], dAp), same("p1-", buf.at[c, B, A], dAm)]
            self.r1 = [
                same("r1+", buf.at[(c, B, Am) + mid + (lo,)], dAp),
                same("r1-", buf.at[(c, B, Ap) + mid + (hi,)], dAm),
            ]
            self.p2 = [same("p2+", buf.at[c, B], dBp), same("p2-", buf.at[c, B], dBm)]
            self.r2 = [
                same("r2+", buf.at[c, Bm, pl.ds(0, 2)], dBp),
                same("r2-", buf.at[c, Bp, pl.ds(2, 2)], dBm),
            ]
            self.s = [same("s%d" % i, buf.at[c, v], sib) for i, v in enumerate((B, Bm, Bp, Bf))]
            self.sent = self.p1 + self.r1 + self.p2 + self.r2 + self.s

        def P1(self):
            self.p1[0].start()
            self.p1[1].start()

        def R1(self):
            for i in (0, 1):
                self.p1[i].wait_recv()
                self.r1[i].start()

        def P2(self):
            self.r1[0].wait_recv()
            self.r1[1].wait_recv()
            self.p2[0].start()
            self.p2[1].start()
            self.s[0].start()

        def R2(self):
            for i in (0, 1):
                self.p2[i].wait_recv()
                self.r2[i].start()
                self.s[1 + i].start()

        def F(self):
            self.r2[0].wait_recv()
            self.r2[1].wait_recv()
            self.s[3].start()

        def G(self):
            for copy in self.s:
                copy.wait_recv()

        def done(self):
            for copy in self.sent:
                copy.wait_send()

    Q, O = Ring("q", bq, 384), Ring("o", bo, 768)
    W1, W2 = Ring("v", b1, 1536), Ring("w", b2, 768)

    own_q = bq.at[c, B, A, :, :, pl.ds(pl.multiple_of(384 * a, 128), 384)]
    own_o = bo.at[c, B, A, :, pl.ds(pl.multiple_of(384 * x, 128), 384)]
    qx = rc("qx", own_q, own_q, dp, far)
    ox = [rc("ox%d" % d, own_o, own_o, dp, mod4(x + d)) for d in (1, 2, 3)]
    gx = [rc("gx%d" % d, xg.at[x], xg.at[x], dp, mod4(x + d)) for d in (1, 2, 3)]
    fn = rc("fn", nsend, nrm.at[x], dp, near)
    fm = rc("fm", nrm.at[x], nrm.at[x], dp, mate)
    fr = rc("fr", nrm.at[near], nrm.at[near], dp, mate)

    own_q[...] = w_qkv[...]
    own_o[...] = w_out[...]
    xg[x] = w_pw[...]
    pl.semaphore_wait(barrier, len(peers))
    qx.start()

    def normed(u, target):
        def step(i, carry):
            rows = pl.ds(pl.multiple_of(i * ROWS, ROWS), ROWS)
            v = norm_rows(frames[u, rows, :].astype(F32), gain_a[...])
            target[rows, :] = v.astype(BF)
            return carry

        lax.fori_loop(0, L // ROWS, step, 0)

    normed(1 - a, nsend)
    fn.start()
    normed(a, nrm.at[x])
    fm.start()
    for copy in ox:
        copy.start()
    for copy in gx:
        copy.start()

    qx.wait_recv()
    Q.P1()
    length = lens[a]
    keys = lax.broadcasted_iota(jnp.int32, (T, 128), 0)
    lane = lax.broadcasted_iota(jnp.int32, (T, 128), 1)
    kbias[...] = jnp.where((keys >= length) & (lane == 0), -1e30, 0.0).astype(BF)
    Q.R1()
    for copy in ox:
        copy.wait_recv()
    O.P1()
    Q.P2()
    fn.wait_recv()
    fr.start()
    for copy in gx:
        copy.wait_recv()

    r = lax.broadcasted_iota(jnp.int32, (48, 64), 0)
    k = lax.broadcasted_iota(jnp.int32, (48, 64), 1)
    pick = ((lax.shift_right_logical(k, 4) * 12 + (k & 15) == r) & ((k & 15) < 12)).astype(F32).astype(BF)
    for n in range(6):
        lanes = slice(768 * n, 768 * n + 768)
        rows = jnp.concatenate([xg[i, :, lanes] for i in range(4)], axis=0)
        rows = jnp.dot(pick, rows, preferred_element_type=F32).astype(BF)
        if n < 4:
            b1[c, B, A, :, lanes] = rows
        else:
            b2[c, B, A, :, 768 * (n - 4) : 768 * (n - 3)] = rows
    W1.P1()
    O.R1()
    Q.R2()
    O.P2()
    W1.R1()
    W2.P1()
    Q.F()
    W1.P2()
    W2.R1()
    Q.G()
    for copy in (fm, fr):
        copy.wait_recv()

    def project(i, carry):
        m, n = lax.div(i, 3), lax.rem(i, 3)
        lanes = pl.ds(pl.multiple_of(n * 256, 256), 256)
        factor = jnp.where(m == 0, SCALE, 1.0).astype(F32)
        w = chunks(bq, lanes, mat=m)
        for j in range(4):
            v = jnp.dot(nrm[j], w, preferred_element_type=F32)
            qkv[m, L * j : L * j + L, lanes] = (v * factor).astype(BF)
        return carry

    lax.fori_loop(0, 9, project, 0)
    O.R2()

    sends = []
    for g in (0, 1):
        cols = pl.ds(pl.multiple_of(384 * (b + 2 * g), 128), 384)
        for d in (1, 2, 3):
            to = mod4(x + d)
            sends.append(
                rc("c%d%d" % (g, d), ctxl.at[to, :, pl.ds(384 * g, 384)], ctx.at[a, :, cols], dp, to)
            )

    QT = 192
    half = lax.broadcasted_iota(jnp.int32, (QT, 128), 1) < HD

    def attend(p, carry):
        lanes = pl.ds(pl.multiple_of(p * 128, 128), 128)
        key = jnp.concatenate([qkv[1, :, lanes], kbias[...]], axis=1)
        value = jnp.concatenate([qkv[2, :, lanes], jnp.ones((T, 128), BF)], axis=1)

        def tile(j, carry):
            rows = pl.ds(pl.multiple_of(j * QT, QT), QT)
            q = qkv[0, rows, lanes]
            results = []
            for h in (0, 1):
                mine = jnp.where(half if h == 0 else ~half, q, jnp.zeros_like(q))
                query = jnp.concatenate([mine, jnp.ones((QT, 128), BF)], axis=1)
                s = lax.dot_general(
                    query, key, (((1,), (1,)), ((), ())), preferred_element_type=F32
                )
                e = jnp.exp2(s - jnp.max(s, -1, keepdims=True)).astype(BF)
                o = jnp.dot(e, value, preferred_element_type=F32)
                results.append(o[:, :128] / o[:, 128:])
            ctxl[j, :, lanes] = jnp.where(half, results[0], results[1]).astype(BF)
            return carry

        lax.fori_loop(0, 4, tile, 0)

        @pl.when(p == 1)
        def _():
            O.F()
            W1.R2()
            W2.P2()

        @pl.when(p == 2)
        def _():
            for copy in sends[:3]:
                copy.start()

        @pl.when(p == 4)
        def _():
            W1.F()

        return carry

    lax.fori_loop(0, 6, attend, 0)
    for copy in sends[3:]:
        copy.start()
    W2.R2()
    for g in (0, 1):
        cols = pl.ds(pl.multiple_of(384 * (b + 2 * g), 128), 384)
        ctx[a, :, cols] = ctxl[x, :, 384 * g : 384 * g + 384]
    O.G()
    for copy in sends:
        copy.wait_recv()

    for n in range(2):
        w = chunks(bo, slice(None), 16 * n, 16)
        for u in (0, 1):
            att = lax.dot_general(
                ctx[u], w, (((1,), (1,)), ((), ())), preferred_element_type=F32
            )
            cols = slice(768 * n, 768 * n + 768)
            res[u, :, cols] = (frames[u, :, cols].astype(F32) + att).astype(BF)

    def norm_conv(i, carry):
        u, rows = lax.div(i, L // ROWS), pl.ds(pl.multiple_of(lax.rem(i, L // ROWS) * ROWS, ROWS), ROWS)
        cin[u, rows, :] = norm_rows(res[u, rows, :].astype(F32), gain_c[...]).astype(BF)
        return carry

    lax.fori_loop(0, 2 * (L // ROWS), norm_conv, 0)
    W2.F()
    W1.G()
    time = x * L + lax.broadcasted_iota(jnp.int32, (L, 256), 0)

    def glu(n, carry):
        lanes = pl.ds(pl.multiple_of(n * 256, 256), 256)
        wv = chunks(b1, lanes)
        wg = chunks(b1, pl.ds(pl.multiple_of(n * 256 + D, 256), 256))
        for u in (0, 1):
            v = jnp.dot(cin[u], wv, preferred_element_type=F32)
            g = jnp.dot(cin[u], wg, preferred_element_type=F32)
            v = jnp.where(time < lens[u], v * sigmoid(g), 0.0)
            gp[u, EDGE : EDGE + L, lanes] = v.astype(BF)
        return carry

    lax.fori_loop(0, 6, glu, 0)
    hp = rc("h+", gp.at[:, pl.ds(L, EDGE)], gp.at[:, pl.ds(0, EDGE)], dp, mod4(x + 1))
    hm = rc("h-", gp.at[:, pl.ds(EDGE, EDGE)], gp.at[:, pl.ds(EDGE + L, EDGE)], dp, mod4(x + 3))
    hp.start()
    hm.start()
    W2.G()
    hp.wait_recv()
    hm.wait_recv()
    first = jnp.where(x == 0, 0.0, 1.0).astype(F32)
    last = jnp.where(x == 3, 0.0, 1.0).astype(F32)

    def conv(i, carry):
        u, n = lax.div(i, 12), lax.rem(i, 12)
        lanes = pl.ds(pl.multiple_of(n * 128, 128), 128)
        cf[0:EDGE, :] = gp[u, 0:EDGE, lanes].astype(F32) * first
        cf[EDGE : EDGE + L, :] = gp[u, EDGE : EDGE + L, lanes].astype(F32)
        cf[EDGE + L :, :] = gp[u, EDGE + L :, lanes].astype(F32) * last
        tap = taps[:, lanes]
        total = jnp.zeros((L, 128), F32)
        for k in range(KERNEL):
            total = total + cf[k + 1 : k + 1 + L, :] * tap[k : k + 1, :]
        dep[u, :, lanes] = total
        return carry

    lax.fori_loop(0, 24, conv, 0)

    def norm_mid(i, carry):
        u, rows = lax.div(i, L // ROWS), pl.ds(pl.multiple_of(lax.rem(i, L // ROWS) * ROWS, ROWS), ROWS)
        h = norm_rows(dep[u, rows, :], gain_m[...])
        cin[u, rows, :] = (h * sigmoid(h)).astype(BF)
        return carry

    lax.fori_loop(0, 2 * (L // ROWS), norm_mid, 0)

    def last_product(n, carry):
        lanes = pl.ds(pl.multiple_of(n * 256, 256), 256)
        w = chunks(b2, lanes)
        for u in (0, 1):
            v = jnp.dot(cin[u], w, preferred_element_type=F32) + res[u, :, lanes].astype(F32)
            out[u, :, lanes] = jnp.where(time < lens[u], v, 0.0).astype(BF)
        return carry

    lax.fori_loop(0, 6, last_product, 0)

    for ring in (Q, O, W1, W2):
        ring.done()
    for copy in [qx] + ox + gx + [fn, fm, fr] + sends + [hp, hm]:
        copy.wait_send()


def local(
    frames, lengths, attn_gain, w_qkv, w_out, conv_gain, w_pw1, depth_kernel, mid_gain, w_pw2
):
    rows = jnp.swapaxes(frames, 0, 1)
    pw = jnp.pad(jnp.concatenate([w_pw1, w_pw2], axis=1), ((0, 4), (0, 0)))
    vmem = pl.BlockSpec(memory_space=pltpu.VMEM)
    result = pl.pallas_call(
        body,
        out_shape=jax.ShapeDtypeStruct((2, L, D), BF),
        in_specs=[pl.BlockSpec(memory_space=pltpu.SMEM)] + [vmem] * 8,
        out_specs=vmem,
        scratch_shapes=[
            pltpu.VMEM((2, 4, 4, 3, 48, 768), BF),
            pltpu.VMEM((2, 4, 4, 48, D), BF),
            pltpu.VMEM((2, 4, 4, 48, 2 * D), BF),
            pltpu.VMEM((2, 4, 4, 48, D), BF),
            pltpu.VMEM((4, 16, 3 * D), BF),
            pltpu.VMEM((4, L, D), BF),
            pltpu.VMEM((L, D), BF),
            pltpu.VMEM((3, T, 768), BF),
            pltpu.VMEM((T, 128), BF),
            pltpu.VMEM((4, L, 768), BF),
            pltpu.VMEM((2, L, D), BF),
            pltpu.VMEM((2, L, D), BF),
            pltpu.VMEM((2, L, D), BF),
            pltpu.VMEM((2, L + 2 * EDGE, D), BF),
            pltpu.VMEM((L + 2 * EDGE, 128), F32),
            pltpu.VMEM((2, L, D), F32),
            pltpu.SemaphoreType.DMA((NSEM,)),
            pltpu.SemaphoreType.DMA((NSEM,)),
        ],
        compiler_params=pltpu.CompilerParams(
            collective_id=0, has_side_effects=True, vmem_limit_bytes=60 * 1024 * 1024
        ),
        name="layer",
    )(
        lengths, rows, attn_gain[None], w_qkv, w_out.T, conv_gain[None], pw, depth_kernel,
        mid_gain[None],
    )
    return jnp.swapaxes(result, 0, 1)


def solution(mesh):
    in_specs = (
        P("seq", "dp", None),
        P("dp"),
        P(),
        P(None, "dp", "seq"),
        P("seq", "dp"),
        P(),
        P(("dp", "seq"), None),
        P(),
        P(),
        P(("dp", "seq"), None),
    )
    out_specs = P("seq", "dp", None)
    return jax.shard_map(local, mesh=mesh, in_specs=in_specs, out_specs=out_specs, check_vma=False)
```

time: 495 us -> 143 us (0.29)
  waiting for transfers between devices: 246 us -> 0 us
  matrix products: 139 us -> 0 us
  Pallas kernels: 0 us -> 130 us
  other arithmetic: 43.6 us -> 1.61 us
  local copies, waits for them, and re-layouts: 42.2 us -> 9.78 us
  between operations: 14.8 us -> 0.01 us
    all_gather x5 -> x0, waiting for transfers between devices: 193 us -> none  [the longest x1 53.1 us: local(): all_frames = lax.all_gather(normed, 'seq', axis=0, tiled=True)]
    dot_general x100 -> x0, matrix products: 139 us -> none  [the longest x48 57.7 us: scores_of(): jnp.einsum('qd,kd->qk', queries, block_keys, preferred_element_type=jnp.f...]
    pallas_call x0 -> x1, Pallas kernels: none -> 130 us  [local(): pl.pallas_call(body, out_shape=jax.ShapeDtypeStruct((2, L, D), BF), in_sp...]
    reduce_scatter x1 -> x0, waiting for transfers between devices: 50.9 us -> none  [local(): lax.psum_scatter(jnp.einsum('tue,ef->tuf', frame_rows, out_cols, preferre...]
    reduce_sum x18 -> x0, other arithmetic: 21.1 us -> none  [the longest x3 14.1 us: layer_norm(): average = jnp.mean(values, -1, keepdims=True)]
    unnamed x18 -> x1, local copies, waits for them, and re-layouts: 22.2 us -> 2.4 us
    lt x25 -> x0, other arithmetic: 15.5 us -> none  [the longest x24 15.4 us: scores_of(): key_inside = first_key + lax.iota(jnp.int32, key_block) < length]
    dynamic_slice x12 -> x0, local copies, waits for them, and re-layouts: 7.3 us -> none  [local(): lax.map(attend, (to_items(qkv[0]), to_items(qkv[1]), to_items(qkv[2]), it...]
  transfers between devices with their start and end apart: 8 -> 0, of which waited for: 5 -> 0; matrix products, arithmetic and copies ran while one was open for 41% -> 0% of each run, Pallas kernels for 0% -> 0%
where the time goes in v1:
time: 143 us; the launch traced here: 141 us
  Pallas kernels  130 us (91%)
  local copies, waits for them, and re-layouts  9.78 us (7%)
  other arithmetic  1.61 us (1%)
    pallas_call x1, Pallas kernels, local(): pl.pallas_call(body, out_shape=jax.ShapeDtypeStruct((2, L, D), BF), in_sp...  130 us
    transpose x1, local copies, waits for them, and re-layouts, local(): return jnp.swapaxes(result, 0, 1)  3.5 us

profile of v1, /device:TPU:1, one launch (start us, length us, event | category | flops | bytes accessed | tf_op | source)
XLA Modules:
  0.0 141.1 jit_solution(5972792082501067379)
XLA Ops:
  0.0 1.3 broadcast_in_dim.9.gain_a
  1.3 1.3 broadcast_in_dim.10.gain_c
  2.6 1.3 broadcast_in_dim.11.gain_m
  3.9 1.6 %fusion.2.w_pw = bf16[16,4608]{1,0:T(8,128)(2,1)} fusion(bf16[12,1536]{1,0:T(8,128)(2,1)} %param.19, bf16[12,3072]{1,0:T(8,128)(2,1)} %param.16), kind=kLoop, calls=%fused_computation.4 | loop fusion | flops 516096 | bytes 258048 | tf_op jit(solution)/shard_map/concatenate | solution.py:372
  5.5 2.4 %copy.14 = bf16[192,2,1536]{2,0,1:T(8,128)(2,1)} copy(bf16[192,2,1536]{2,1,0:T(2,128)(2,1)} %param.10) | data formatting | bytes 2359296 | tf_op args[0]
  7.9 129.7 %layer.1 = bf16[2,192,1536]{2,1,0:T(8,128)(2,1)} custom-call(s32[2]{0:T(128)} %lens.1, bf16[2,192,1536]{2,1,0:T(8,128)(2,1)} %bitcast.6, f32[1,1536]{1,0:T(1,128)} %broadcast_in_dim.9.gain_a, bf16[3,48,384]{2,1,0:T(8,128)(2,1)} %w_qkv.1, bf16[48,384]{1,0:T(8,128)(2,1)} %bitcast.7, f32[1,1536]{1,0:T(1,128)} %broadcast_in_dim.10.gain_c, ...), custom_call_target="tpu_custom_call" | custom-call | tf_op jit(solution)/shard_map/layer/pallas_call | solution.py:374
  137.6 3.5 %copy.12 = bf16[192,2,1536]{2,1,0:T(2,128)(2,1)} copy(bf16[192,2,1536]{2,0,1:T(8,128)(2,1)} %bitcast.5) | data formatting | bytes 2359296 | tf_op jit(solution)/shard_map/transpose | solution.py:407

commit v2 on v1

--- a/solution.py
+++ b/solution.py
@@ -16,8 +16,8 @@
 BF = jnp.bfloat16
 F32 = jnp.float32
 SCALE = 1.4426950408889634 / 8.0
-NSEM = 96
-ROWS = 32
+NSEM = 112
+ROWS = 96
 
 
 def sigmoid(v):
@@ -43,17 +43,19 @@
 
 
 def body(
-    lens, frames, gain_a, w_qkv, w_out, gain_c, w_pw, taps, gain_m, out,
+    lens, frames, gain_a, w_qkv, w_out, gain_c, w_pw1, w_pw2, taps, gain_m, out,
     bq, bo, b1, b2, xg, nrm, nsend, qkv, kbias, ctxl, ctx, res, cin, gp, cf, dep, send, recv,
 ):
     x = lax.axis_index("seq")
     dp = lax.axis_index("dp")
     z, y, c = lax.div(dp, 8), lax.rem(lax.div(dp, 2), 4), lax.rem(dp, 2)
-    a, b = lax.div(x, 2), lax.rem(x, 2)
 
     def mod4(v):
         return lax.rem(v, 4)
 
+    xc = mod4(x + c)
+    a, b, hi = lax.div(xc, 2), lax.rem(x, 2), lax.div(x, 2)
+
     A = (1 - c) * y + c * z
     B = (1 - c) * z + c * y
 
@@ -62,8 +64,10 @@
 
     Ap, Am, Bp, Bm, Bf = mod4(A + 1), mod4(A + 3), mod4(B + 1), mod4(B + 3), mod4(B + 2)
     dAp, dAm, dBp, dBm = dev(B, Ap), dev(B, Am), dev(Bp, A), dev(Bm, A)
+    dAf = dev(B, mod4(A + 2))
     sib = dp + 1 - 2 * c
-    near, mate, far = 3 - x, x + 1 - 2 * b, mod4(x + 2)
+    near, mate = mod4(7 - xc - c), mod4(xc + 5 - 2 * lax.rem(xc, 2) - c)
+    far = mod4(x + 2)
 
     names = {}
 
@@ -76,31 +80,42 @@
 
     barrier = pltpu.get_barrier_semaphore()
     peers = [(dp, mod4(x + d)) for d in (1, 2, 3)]
-    peers += [(d, x) for d in (dAp, dAm, dBp, dBm, sib)]
+    peers += [(d, x) for d in (dAp, dAm, dAf, dBp, dBm, sib)]
     for peer in peers:
         pl.semaphore_signal(barrier, inc=1, device_id=peer, device_id_type=pl.DeviceIdType.MESH)
 
     class Ring:
-        def __init__(self, key, buf, half):
+        def __init__(self, key, buf, half, direct=False):
             same = lambda n, ref, to: rc(key + n, ref, ref, to, x)
-            lo, hi = pl.ds(0, half), pl.ds(half, half)
+            lo, hi_ = pl.ds(0, half), pl.ds(half, half)
             mid = (slice(None),) * (len(buf.shape) - 4)
-            self.p1 = [same("p1+", buf.at[c, B, A], dAp), same("p1-", buf.at[c, B, A], dAm)]
-            self.r1 = [
-                same("r1+", buf.at[(c, B, Am) + mid + (lo,)], dAp),
-                same("r1-", buf.at[(c, B, Ap) + mid + (hi,)], dAm),
+            if direct:
+                self.p1, self.r1 = [], []
+                for n, v in (("own", hi), ("far", 1 - hi)):
+                    at = pl.ds(pl.multiple_of(v * half, 128), half)
+                    ref = buf.at[(c, B, A) + mid + (at,)]
+                    for m, to in (("+", dAp), ("-", dAm), ("2", dAf)):
+                        self.p1.append(same(n + m, ref, to))
+            else:
+                self.p1 = [same("p1+", buf.at[c, B, A], dAp), same("p1-", buf.at[c, B, A], dAm)]
+                self.r1 = [
+                    same("r1+", buf.at[(c, B, Am) + mid + (lo,)], dAp),
+                    same("r1-", buf.at[(c, B, Ap) + mid + (hi_,)], dAm),
+                ]
+            first, second = pl.ds(0, 2), pl.ds(2, 2)
+            self.p2 = [
+                same("p2a+", buf.at[c, B, first], dBp), same("p2a-", buf.at[c, B, second], dBm),
+                same("p2b+", buf.at[c, B, second], dBp), same("p2b-", buf.at[c, B, first], dBm),
             ]
-            self.p2 = [same("p2+", buf.at[c, B], dBp), same("p2-", buf.at[c, B], dBm)]
             self.r2 = [
-                same("r2+", buf.at[c, Bm, pl.ds(0, 2)], dBp),
-                same("r2-", buf.at[c, Bp, pl.ds(2, 2)], dBm),
+                same("r2+", buf.at[c, Bm, first], dBp), same("r2-", buf.at[c, Bp, second], dBm),
             ]
             self.s = [same("s%d" % i, buf.at[c, v], sib) for i, v in enumerate((B, Bm, Bp, Bf))]
             self.sent = self.p1 + self.r1 + self.p2 + self.r2 + self.s
 
-        def P1(self):
-            self.p1[0].start()
-            self.p1[1].start()
+        def P1(self, first=0, count=2):
+            for copy in self.p1[first : first + count]:
+                copy.start()
 
         def R1(self):
             for i in (0, 1):
@@ -108,16 +123,20 @@
                 self.r1[i].start()
 
         def P2(self):
-            self.r1[0].wait_recv()
-            self.r1[1].wait_recv()
-            self.p2[0].start()
-            self.p2[1].start()
+            for copy in self.r1 or self.p1:
+                copy.wait_recv()
+            for copy in self.p2:
+                copy.start()
             self.s[0].start()
 
         def R2(self):
             for i in (0, 1):
                 self.p2[i].wait_recv()
                 self.r2[i].start()
+
+        def S2(self):
+            for i in (0, 1):
+                self.p2[2 + i].wait_recv()
                 self.s[1 + i].start()
 
         def F(self):
@@ -133,10 +152,10 @@
             for copy in self.sent:
                 copy.wait_send()
 
-    Q, O = Ring("q", bq, 384), Ring("o", bo, 768)
+    Q, O = Ring("q", bq, 384, True), Ring("o", bo, 768)
     W1, W2 = Ring("v", b1, 1536), Ring("w", b2, 768)
 
-    own_q = bq.at[c, B, A, :, :, pl.ds(pl.multiple_of(384 * a, 128), 384)]
+    own_q = bq.at[c, B, A, :, :, pl.ds(pl.multiple_of(384 * hi, 128), 384)]
     own_o = bo.at[c, B, A, :, pl.ds(pl.multiple_of(384 * x, 128), 384)]
     qx = rc("qx", own_q, own_q, dp, far)
     ox = [rc("ox%d" % d, own_o, own_o, dp, mod4(x + d)) for d in (1, 2, 3)]
@@ -147,14 +166,19 @@
 
     own_q[...] = w_qkv[...]
     own_o[...] = w_out[...]
-    xg[x] = w_pw[...]
+    xg[x] = jnp.zeros((16, 3 * D), BF)
+    xg[x, 0:12, 0 : 2 * D] = w_pw1[...]
+    xg[x, 0:12, 2 * D :] = w_pw2[...]
     pl.semaphore_wait(barrier, len(peers))
     qx.start()
+    Q.P1(0, 3)
+    for copy in ox + gx:
+        copy.start()
 
     def normed(u, target):
         def step(i, carry):
             rows = pl.ds(pl.multiple_of(i * ROWS, ROWS), ROWS)
-            v = norm_rows(frames[u, rows, :].astype(F32), gain_a[...])
+            v = norm_rows(frames[u, rows, :].astype(F32), gain_a[...][None])
             target[rows, :] = v.astype(BF)
             return carry
 
@@ -164,24 +188,19 @@
     fn.start()
     normed(a, nrm.at[x])
     fm.start()
-    for copy in ox:
-        copy.start()
-    for copy in gx:
-        copy.start()
-
     qx.wait_recv()
-    Q.P1()
+    Q.P1(3, 3)
     length = lens[a]
     keys = lax.broadcasted_iota(jnp.int32, (T, 128), 0)
     lane = lax.broadcasted_iota(jnp.int32, (T, 128), 1)
     kbias[...] = jnp.where((keys >= length) & (lane == 0), -1e30, 0.0).astype(BF)
-    Q.R1()
     for copy in ox:
         copy.wait_recv()
     O.P1()
     Q.P2()
     fn.wait_recv()
     fr.start()
+    O.R1()
     for copy in gx:
         copy.wait_recv()
 
@@ -196,15 +215,12 @@
             b1[c, B, A, :, lanes] = rows
         else:
             b2[c, B, A, :, 768 * (n - 4) : 768 * (n - 3)] = rows
+    Q.R2()
     W1.P1()
-    O.R1()
-    Q.R2()
+    W2.P1()
     O.P2()
-    W1.R1()
-    W2.P1()
+    Q.S2()
     Q.F()
-    W1.P2()
-    W2.R1()
     Q.G()
     for copy in (fm, fr):
         copy.wait_recv()
@@ -217,19 +233,27 @@
         for j in range(4):
             v = jnp.dot(nrm[j], w, preferred_element_type=F32)
             qkv[m, L * j : L * j + L, lanes] = (v * factor).astype(BF)
+
+        @pl.when(i == 4)
+        def _():
+            W1.R1()
+            W2.R1()
+
         return carry
 
     lax.fori_loop(0, 9, project, 0)
     O.R2()
 
-    sends = []
-    for g in (0, 1):
-        cols = pl.ds(pl.multiple_of(384 * (b + 2 * g), 128), 384)
-        for d in (1, 2, 3):
-            to = mod4(x + d)
-            sends.append(
-                rc("c%d%d" % (g, d), ctxl.at[to, :, pl.ds(384 * g, 384)], ctx.at[a, :, cols], dp, to)
-            )
+    def send_pair(p, d):
+        to = mod4(x + d)
+        block = b + 2 * lax.div(p, 3)
+        cols = pl.ds(pl.multiple_of(384 * block + 128 * lax.rem(p, 3), 128), 128)
+        i = 80 + 3 * p + d - 1
+        return pltpu.make_async_remote_copy(
+            src_ref=ctxl.at[to, :, pl.ds(pl.multiple_of(p * 128, 128), 128)],
+            dst_ref=ctx.at[a, :, cols], send_sem=send.at[i], recv_sem=recv.at[i],
+            device_id=(dp, to), device_id_type=pl.DeviceIdType.MESH,
+        )
 
     QT = 192
     half = lax.broadcasted_iota(jnp.int32, (QT, 128), 1) < HD
@@ -255,35 +279,36 @@
             ctxl[j, :, lanes] = jnp.where(half, results[0], results[1]).astype(BF)
             return carry
 
-        lax.fori_loop(0, 4, tile, 0)
+        lax.fori_loop(0, 4, tile, 0, unroll=4)
+
+        for d in (2, 1, 3):
+            send_pair(p, d).start()
 
         @pl.when(p == 1)
         def _():
+            W1.P2()
+            O.S2()
             O.F()
+
+        @pl.when(p == 4)
+        def _():
             W1.R2()
             W2.P2()
 
-        @pl.when(p == 2)
-        def _():
-            for copy in sends[:3]:
-                copy.start()
-
-        @pl.when(p == 4)
-        def _():
-            W1.F()
-
         return carry
 
     lax.fori_loop(0, 6, attend, 0)
-    for copy in sends[3:]:
-        copy.start()
-    W2.R2()
     for g in (0, 1):
         cols = pl.ds(pl.multiple_of(384 * (b + 2 * g), 128), 384)
         ctx[a, :, cols] = ctxl[x, :, 384 * g : 384 * g + 384]
     O.G()
-    for copy in sends:
-        copy.wait_recv()
+
+    def arrive(p, carry):
+        for d in (1, 2, 3):
+            send_pair(p, d).wait_recv()
+        return carry
+
+    lax.fori_loop(0, 6, arrive, 0)
 
     for n in range(2):
         w = chunks(bo, slice(None), 16 * n, 16)
@@ -296,11 +321,12 @@
 
     def norm_conv(i, carry):
         u, rows = lax.div(i, L // ROWS), pl.ds(pl.multiple_of(lax.rem(i, L // ROWS) * ROWS, ROWS), ROWS)
-        cin[u, rows, :] = norm_rows(res[u, rows, :].astype(F32), gain_c[...]).astype(BF)
+        cin[u, rows, :] = norm_rows(res[u, rows, :].astype(F32), gain_c[...][None]).astype(BF)
         return carry
 
     lax.fori_loop(0, 2 * (L // ROWS), norm_conv, 0)
-    W2.F()
+    W1.S2()
+    W1.F()
     W1.G()
     time = x * L + lax.broadcasted_iota(jnp.int32, (L, 256), 0)
 
@@ -313,6 +339,11 @@
             g = jnp.dot(cin[u], wg, preferred_element_type=F32)
             v = jnp.where(time < lens[u], v * sigmoid(g), 0.0)
             gp[u, EDGE : EDGE + L, lanes] = v.astype(BF)
+
+        @pl.when(n == 2)
+        def _():
+            W2.R2()
+
         return carry
 
     lax.fori_loop(0, 6, glu, 0)
@@ -320,7 +351,7 @@
     hm = rc("h-", gp.at[:, pl.ds(EDGE, EDGE)], gp.at[:, pl.ds(EDGE + L, EDGE)], dp, mod4(x + 3))
     hp.start()
     hm.start()
-    W2.G()
+    W2.S2()
     hp.wait_recv()
     hm.wait_recv()
     first = jnp.where(x == 0, 0.0, 1.0).astype(F32)
@@ -340,14 +371,17 @@
         return carry
 
     lax.fori_loop(0, 24, conv, 0)
+    W2.F()
 
     def norm_mid(i, carry):
         u, rows = lax.div(i, L // ROWS), pl.ds(pl.multiple_of(lax.rem(i, L // ROWS) * ROWS, ROWS), ROWS)
-        h = norm_rows(dep[u, rows, :], gain_m[...])
+        h = norm_rows(dep[u, rows, :], gain_m[...][None])
         cin[u, rows, :] = (h * sigmoid(h)).astype(BF)
         return carry
 
     lax.fori_loop(0, 2 * (L // ROWS), norm_mid, 0)
+
+    W2.G()
 
     def last_product(n, carry):
         lanes = pl.ds(pl.multiple_of(n * 256, 256), 256)
@@ -361,20 +395,26 @@
 
     for ring in (Q, O, W1, W2):
         ring.done()
-    for copy in [qx] + ox + gx + [fn, fm, fr] + sends + [hp, hm]:
+    for copy in [qx] + ox + gx + [fn, fm, fr, hp, hm]:
         copy.wait_send()
+
+    def leave(p, carry):
+        for d in (1, 2, 3):
+            send_pair(p, d).wait_send()
+        return carry
+
+    lax.fori_loop(0, 6, leave, 0)
 
 
 def local(
     frames, lengths, attn_gain, w_qkv, w_out, conv_gain, w_pw1, depth_kernel, mid_gain, w_pw2
 ):
     rows = jnp.swapaxes(frames, 0, 1)
-    pw = jnp.pad(jnp.concatenate([w_pw1, w_pw2], axis=1), ((0, 4), (0, 0)))
     vmem = pl.BlockSpec(memory_space=pltpu.VMEM)
     result = pl.pallas_call(
         body,
         out_shape=jax.ShapeDtypeStruct((2, L, D), BF),
-        in_specs=[pl.BlockSpec(memory_space=pltpu.SMEM)] + [vmem] * 8,
+        in_specs=[pl.BlockSpec(memory_space=pltpu.SMEM)] + [vmem] * 9,
         out_specs=vmem,
         scratch_shapes=[
             pltpu.VMEM((2, 4, 4, 3, 48, 768), BF),
@@ -401,8 +441,7 @@
         ),
         name="layer",
     )(
-        lengths, rows, attn_gain[None], w_qkv, w_out.T, conv_gain[None], pw, depth_kernel,
-        mid_gain[None],
+        lengths, rows, attn_gain, w_qkv, w_out.T, conv_gain, w_pw1, w_pw2, depth_kernel, mid_gain,
     )
     return jnp.swapaxes(result, 0, 1)
 

time: 143 us -> 119 us (0.83); the launches traced: 141 us -> 119 us
  Pallas kernels: 130 us -> 113 us
  local copies, waits for them, and re-layouts: 9.78 us -> 5.9 us
  other arithmetic: 1.61 us -> 0 us
    pallas_call x1, Pallas kernels: 130 us -> 113 us  [local(): pl.pallas_call(body, out_shape=jax.ShapeDtypeStruct((2, L, D), BF), in_sp...]
    broadcast_in_dim x3 -> x0, local copies, waits for them, and re-layouts: 3.88 us -> none  [the longest x1 1.3 us: local(): mid_gain[None]]
    concatenate x1 -> x0, other arithmetic: 1.61 us -> none  [local(): pw = jnp.pad(jnp.concatenate([w_pw1, w_pw2], axis=1), ((0, 4), (0, 0)))]
where the time goes in v2:
time: 119 us
  Pallas kernels  113 us (95%)
  local copies, waits for them, and re-layouts  5.9 us (5%)
    pallas_call x1, Pallas kernels, local(): pl.pallas_call(body, out_shape=jax.ShapeDtypeStruct((2, L, D), BF), in_sp...  113 us
    transpose x1, local copies, waits for them, and re-layouts, local(): return jnp.swapaxes(result, 0, 1)  3.5 us
    unnamed x1, local copies, waits for them, and re-layouts  2.4 us

profile of v2, /device:TPU:1, one launch (start us, length us, event | category | flops | bytes accessed | tf_op | source)
XLA Modules:
  0.0 118.7 jit_solution(9735269331958512944)
XLA Ops:
  0.0 2.4 %copy.14 = bf16[192,2,1536]{2,0,1:T(8,128)(2,1)} copy(bf16[192,2,1536]{2,1,0:T(2,128)(2,1)} %param.10) | data formatting | bytes 2359296 | tf_op args[0]
  2.4 112.8 %layer.1 = bf16[2,192,1536]{2,1,0:T(8,128)(2,1)} custom-call(s32[2]{0:T(128)} %lens.1, bf16[2,192,1536]{2,1,0:T(8,128)(2,1)} %bitcast.6, f32[1536]{0:T(1024)} %gain_a.1, bf16[3,48,384]{2,1,0:T(8,128)(2,1)} %w_qkv.1, bf16[48,384]{1,0:T(8,128)(2,1)} %bitcast.7, f32[1536]{0:T(1024)} %gain_c.1, bf16[12,3072]{1,0:T(8,128)(2,1)} %w_pw1.1, bf16[12,1536]{1,0:T(8,128)(2,1)} %w_pw2.1, ...), custom_call_target="tpu_custom_call" | custom-call | tf_op jit(solution)/shard_map/layer/pallas_call | solution.py:414
  115.2 3.5 %copy.12 = bf16[192,2,1536]{2,1,0:T(2,128)(2,1)} copy(bf16[192,2,1536]{2,0,1:T(8,128)(2,1)} %bitcast.5) | data formatting | bytes 2359296 | tf_op jit(solution)/shard_map/transpose | solution.py:446

commit v3 on v2

--- a/solution.py
+++ b/solution.py
@@ -17,7 +17,8 @@
 F32 = jnp.float32
 SCALE = 1.4426950408889634 / 8.0
 NSEM = 112
-ROWS = 96
+QT = 384
+ROWS = 192
 
 
 def sigmoid(v):
@@ -37,7 +38,7 @@
         z, y, c = i // 8, (i // 2) % 4, i % 2
         where = (c, z, y) if c == 0 else (c, y, z)
         if mat is not None:
-            where = where + (mat,)
+            where = (mat[0],) + where + (mat[1],)
         out.append(buf[where + (slice(None), lanes)])
     return jnp.concatenate(out, axis=0)
 
@@ -54,7 +55,7 @@
         return lax.rem(v, 4)
 
     xc = mod4(x + c)
-    a, b, hi = lax.div(xc, 2), lax.rem(x, 2), lax.div(x, 2)
+    a = lax.div(xc, 2)
 
     A = (1 - c) * y + c * z
     B = (1 - c) * z + c * y
@@ -90,12 +91,11 @@
             lo, hi_ = pl.ds(0, half), pl.ds(half, half)
             mid = (slice(None),) * (len(buf.shape) - 4)
             if direct:
-                self.p1, self.r1 = [], []
-                for n, v in (("own", hi), ("far", 1 - hi)):
-                    at = pl.ds(pl.multiple_of(v * half, 128), half)
-                    ref = buf.at[(c, B, A) + mid + (at,)]
-                    for m, to in (("+", dAp), ("-", dAm), ("2", dAf)):
-                        self.p1.append(same(n + m, ref, to))
+                self.r1 = []
+                self.p1 = [
+                    same("p1" + m, buf.at[c, B, A], to)
+                    for m, to in (("+", dAp), ("-", dAm), ("2", dAf))
+                ]
             else:
                 self.p1 = [same("p1+", buf.at[c, B, A], dAp), same("p1-", buf.at[c, B, A], dAm)]
                 self.r1 = [
@@ -113,8 +113,8 @@
             self.s = [same("s%d" % i, buf.at[c, v], sib) for i, v in enumerate((B, Bm, Bp, Bf))]
             self.sent = self.p1 + self.r1 + self.p2 + self.r2 + self.s
 
-        def P1(self, first=0, count=2):
-            for copy in self.p1[first : first + count]:
+        def P1(self):
+            for copy in self.p1:
                 copy.start()
 
         def R1(self):
@@ -152,14 +152,17 @@
             for copy in self.sent:
                 copy.wait_send()
 
-    Q, O = Ring("q", bq, 384, True), Ring("o", bo, 768)
+    QA, QB = Ring("q", bq.at[0], 0, True), Ring("r", bq.at[1], 0, True)
+    O = Ring("o", bo, 768)
     W1, W2 = Ring("v", b1, 1536), Ring("w", b2, 768)
 
-    own_q = bq.at[c, B, A, :, :, pl.ds(pl.multiple_of(384 * hi, 128), 384)]
+    own_q = bq.at[0, c, B, A]
     own_o = bo.at[c, B, A, :, pl.ds(pl.multiple_of(384 * x, 128), 384)]
-    qx = rc("qx", own_q, own_q, dp, far)
+    qx = rc("qx", own_q, bq.at[1, c, B, A], dp, far)
     ox = [rc("ox%d" % d, own_o, own_o, dp, mod4(x + d)) for d in (1, 2, 3)]
-    gx = [rc("gx%d" % d, xg.at[x], xg.at[x], dp, mod4(x + d)) for d in (1, 2, 3)]
+    parts = [xg.at[x, :, pl.ds(0, 2 * D)], xg.at[x, :, pl.ds(2 * D, D)]]
+    g1 = [rc("g1%d" % d, parts[0], parts[0], dp, mod4(x + d)) for d in (1, 2, 3)]
+    g2 = [rc("g2%d" % d, parts[1], parts[1], dp, mod4(x + d)) for d in (1, 2, 3)]
     fn = rc("fn", nsend, nrm.at[x], dp, near)
     fm = rc("fm", nrm.at[x], nrm.at[x], dp, mate)
     fr = rc("fr", nrm.at[near], nrm.at[near], dp, mate)
@@ -171,8 +174,8 @@
     xg[x, 0:12, 2 * D :] = w_pw2[...]
     pl.semaphore_wait(barrier, len(peers))
     qx.start()
-    Q.P1(0, 3)
-    for copy in ox + gx:
+    QA.P1()
+    for copy in ox + g1:
         copy.start()
 
     def normed(u, target):
@@ -188,74 +191,79 @@
     fn.start()
     normed(a, nrm.at[x])
     fm.start()
+    QA.P2()
     qx.wait_recv()
-    Q.P1(3, 3)
+    QB.P1()
     length = lens[a]
     keys = lax.broadcasted_iota(jnp.int32, (T, 128), 0)
     lane = lax.broadcasted_iota(jnp.int32, (T, 128), 1)
     kbias[...] = jnp.where((keys >= length) & (lane == 0), -1e30, 0.0).astype(BF)
+    QA.R2()
+    QB.P2()
     for copy in ox:
         copy.wait_recv()
     O.P1()
-    Q.P2()
-    fn.wait_recv()
-    fr.start()
-    O.R1()
-    for copy in gx:
+    QA.S2()
+    QB.R2()
+    for copy in g1:
         copy.wait_recv()
 
     r = lax.broadcasted_iota(jnp.int32, (48, 64), 0)
     k = lax.broadcasted_iota(jnp.int32, (48, 64), 1)
     pick = ((lax.shift_right_logical(k, 4) * 12 + (k & 15) == r) & ((k & 15) < 12)).astype(F32).astype(BF)
-    for n in range(6):
-        lanes = slice(768 * n, 768 * n + 768)
-        rows = jnp.concatenate([xg[i, :, lanes] for i in range(4)], axis=0)
-        rows = jnp.dot(pick, rows, preferred_element_type=F32).astype(BF)
-        if n < 4:
-            b1[c, B, A, :, lanes] = rows
-        else:
-            b2[c, B, A, :, 768 * (n - 4) : 768 * (n - 3)] = rows
-    Q.R2()
+
+    def assemble(first, count, target):
+        for n in range(count):
+            lanes = slice(768 * (first + n), 768 * (first + n) + 768)
+            rows = jnp.concatenate([xg[i, :, lanes] for i in range(4)], axis=0)
+            rows = jnp.dot(pick, rows, preferred_element_type=F32).astype(BF)
+            target[c, B, A, :, 768 * n : 768 * n + 768] = rows
+
+    assemble(0, 4, b1)
     W1.P1()
-    W2.P1()
+    O.R1()
+    fn.wait_recv()
+    fr.start()
+    for copy in g2:
+        copy.start()
+    QA.F()
     O.P2()
-    Q.S2()
-    Q.F()
-    Q.G()
+    W1.R1()
+    QB.S2()
+    QB.F()
+    QA.G()
     for copy in (fm, fr):
         copy.wait_recv()
 
-    def project(i, carry):
-        m, n = lax.div(i, 3), lax.rem(i, 3)
-        lanes = pl.ds(pl.multiple_of(n * 256, 256), 256)
-        factor = jnp.where(m == 0, SCALE, 1.0).astype(F32)
-        w = chunks(bq, lanes, mat=m)
-        for j in range(4):
-            v = jnp.dot(nrm[j], w, preferred_element_type=F32)
-            qkv[m, L * j : L * j + L, lanes] = (v * factor).astype(BF)
-
-        @pl.when(i == 4)
-        def _():
-            W1.R1()
-            W2.R1()
-
-        return carry
-
-    lax.fori_loop(0, 9, project, 0)
+    def project(g):
+        def step(m, carry):
+            factor = jnp.where(m == 0, SCALE, 1.0).astype(F32)
+            w = chunks(bq, slice(None), mat=(g, m))
+            v = jnp.dot(nrm[...].reshape(T, D), w, preferred_element_type=F32)
+            qkv[m, :, 384 * g : 384 * g + 384] = (v * factor).astype(BF)
+            return carry
+
+        lax.fori_loop(0, 3, step, 0)
+
+    project(0)
+    for copy in g2:
+        copy.wait_recv()
+    assemble(4, 2, b2)
+    W2.P1()
     O.R2()
+    W1.P2()
 
     def send_pair(p, d):
         to = mod4(x + d)
-        block = b + 2 * lax.div(p, 3)
+        block = mod4(x + 2 * lax.div(p, 3))
         cols = pl.ds(pl.multiple_of(384 * block + 128 * lax.rem(p, 3), 128), 128)
-        i = 80 + 3 * p + d - 1
+        i = 94 + 3 * p + d - 1
         return pltpu.make_async_remote_copy(
-            src_ref=ctxl.at[to, :, pl.ds(pl.multiple_of(p * 128, 128), 128)],
+            src_ref=ctxl.at[pl.ds(pl.multiple_of(to * L, L), L), pl.ds(pl.multiple_of(p * 128, 128), 128)],
             dst_ref=ctx.at[a, :, cols], send_sem=send.at[i], recv_sem=recv.at[i],
             device_id=(dp, to), device_id_type=pl.DeviceIdType.MESH,
         )
 
-    QT = 192
     half = lax.broadcasted_iota(jnp.int32, (QT, 128), 1) < HD
 
     def attend(p, carry):
@@ -276,31 +284,37 @@
                 e = jnp.exp2(s - jnp.max(s, -1, keepdims=True)).astype(BF)
                 o = jnp.dot(e, value, preferred_element_type=F32)
                 results.append(o[:, :128] / o[:, 128:])
-            ctxl[j, :, lanes] = jnp.where(half, results[0], results[1]).astype(BF)
+            ctxl[rows, lanes] = jnp.where(half, results[0], results[1]).astype(BF)
             return carry
 
-        lax.fori_loop(0, 4, tile, 0, unroll=4)
+        lax.fori_loop(0, T // QT, tile, 0, unroll=T // QT)
 
         for d in (2, 1, 3):
             send_pair(p, d).start()
 
-        @pl.when(p == 1)
+        @pl.when(p == 0)
         def _():
-            W1.P2()
+            W2.R1()
+
+        @pl.when(p == 2)
+        def _():
             O.S2()
             O.F()
 
-        @pl.when(p == 4)
+        @pl.when(p == 3)
         def _():
             W1.R2()
             W2.P2()
 
         return carry
 
-    lax.fori_loop(0, 6, attend, 0)
+    lax.fori_loop(0, 3, attend, 0)
+    QB.G()
+    project(1)
+    lax.fori_loop(3, 6, attend, 0)
     for g in (0, 1):
-        cols = pl.ds(pl.multiple_of(384 * (b + 2 * g), 128), 384)
-        ctx[a, :, cols] = ctxl[x, :, 384 * g : 384 * g + 384]
+        cols = pl.ds(pl.multiple_of(384 * mod4(x + 2 * g), 128), 384)
+        ctx[a, :, cols] = ctxl[pl.ds(pl.multiple_of(x * L, L), L), 384 * g : 384 * g + 384]
     O.G()
 
     def arrive(p, carry):
@@ -312,12 +326,12 @@
 
     for n in range(2):
         w = chunks(bo, slice(None), 16 * n, 16)
-        for u in (0, 1):
-            att = lax.dot_general(
-                ctx[u], w, (((1,), (1,)), ((), ())), preferred_element_type=F32
-            )
-            cols = slice(768 * n, 768 * n + 768)
-            res[u, :, cols] = (frames[u, :, cols].astype(F32) + att).astype(BF)
+        cols = slice(768 * n, 768 * n + 768)
+        att = lax.dot_general(
+            ctx[...].reshape(2 * L, D), w, (((1,), (1,)), ((), ())), preferred_element_type=F32
+        )
+        total = frames[:, :, cols].astype(F32) + att.reshape(2, L, 768)
+        res[:, :, cols] = total.astype(BF)
 
     def norm_conv(i, carry):
         u, rows = lax.div(i, L // ROWS), pl.ds(pl.multiple_of(lax.rem(i, L // ROWS) * ROWS, ROWS), ROWS)
@@ -334,11 +348,12 @@
         lanes = pl.ds(pl.multiple_of(n * 256, 256), 256)
         wv = chunks(b1, lanes)
         wg = chunks(b1, pl.ds(pl.multiple_of(n * 256 + D, 256), 256))
+        rows = cin[...].reshape(2 * L, D)
+        v = jnp.dot(rows, wv, preferred_element_type=F32)
+        g = jnp.dot(rows, wg, preferred_element_type=F32)
+        v = (v * sigmoid(g)).reshape(2, L, 256)
         for u in (0, 1):
-            v = jnp.dot(cin[u], wv, preferred_element_type=F32)
-            g = jnp.dot(cin[u], wg, preferred_element_type=F32)
-            v = jnp.where(time < lens[u], v * sigmoid(g), 0.0)
-            gp[u, EDGE : EDGE + L, lanes] = v.astype(BF)
+            gp[u, EDGE : EDGE + L, lanes] = jnp.where(time < lens[u], v[u], 0.0).astype(BF)
 
         @pl.when(n == 2)
         def _():
@@ -386,16 +401,17 @@
     def last_product(n, carry):
         lanes = pl.ds(pl.multiple_of(n * 256, 256), 256)
         w = chunks(b2, lanes)
+        v = jnp.dot(cin[...].reshape(2 * L, D), w, preferred_element_type=F32).reshape(2, L, 256)
         for u in (0, 1):
-            v = jnp.dot(cin[u], w, preferred_element_type=F32) + res[u, :, lanes].astype(F32)
-            out[u, :, lanes] = jnp.where(time < lens[u], v, 0.0).astype(BF)
+            total = v[u] + res[u, :, lanes].astype(F32)
+            out[u, :, lanes] = jnp.where(time < lens[u], total, 0.0).astype(BF)
         return carry
 
     lax.fori_loop(0, 6, last_product, 0)
 
-    for ring in (Q, O, W1, W2):
+    for ring in (QA, QB, O, W1, W2):
         ring.done()
-    for copy in [qx] + ox + gx + [fn, fm, fr, hp, hm]:
+    for copy in [qx] + ox + g1 + g2 + [fn, fm, fr, hp, hm]:
         copy.wait_send()
 
     def leave(p, carry):
@@ -417,7 +433,7 @@
         in_specs=[pl.BlockSpec(memory_space=pltpu.SMEM)] + [vmem] * 9,
         out_specs=vmem,
         scratch_shapes=[
-            pltpu.VMEM((2, 4, 4, 3, 48, 768), BF),
+            pltpu.VMEM((2, 2, 4, 4, 3, 48, 384), BF),
             pltpu.VMEM((2, 4, 4, 48, D), BF),
             pltpu.VMEM((2, 4, 4, 48, 2 * D), BF),
             pltpu.VMEM((2, 4, 4, 48, D), BF),
@@ -426,7 +442,7 @@
             pltpu.VMEM((L, D), BF),
             pltpu.VMEM((3, T, 768), BF),
             pltpu.VMEM((T, 128), BF),
-            pltpu.VMEM((4, L, 768), BF),
+            pltpu.VMEM((T, 768), BF),
             pltpu.VMEM((2, L, D), BF),
             pltpu.VMEM((2, L, D), BF),
             pltpu.VMEM((2, L, D), BF),

time: 119 us -> 107 us (0.90)
  Pallas kernels: 113 us -> 101 us
    pallas_call x1, Pallas kernels: 113 us -> 101 us  [local(): pl.pallas_call(body, out_shape=jax.ShapeDtypeStruct((2, L, D), BF), in_sp...]
where the time goes in v3:
time: 107 us
  Pallas kernels  101 us (94%)
  local copies, waits for them, and re-layouts  5.9 us (6%)
    pallas_call x1, Pallas kernels, local(): pl.pallas_call(body, out_shape=jax.ShapeDtypeStruct((2, L, D), BF), in_sp...  101 us
    transpose x1, local copies, waits for them, and re-layouts, local(): return jnp.swapaxes(result, 0, 1)  3.5 us
    unnamed x1, local copies, waits for them, and re-layouts  2.4 us

profile of v3, /device:TPU:1, one launch (start us, length us, event | category | flops | bytes accessed | tf_op | source)
XLA Modules:
  0.0 106.6 jit_solution(17081118473326169893)
XLA Ops:
  0.0 2.4 %copy.14 = bf16[192,2,1536]{2,0,1:T(8,128)(2,1)} copy(bf16[192,2,1536]{2,1,0:T(2,128)(2,1)} %param.10) | data formatting | bytes 2359296 | tf_op args[0]
  2.4 100.7 %layer.1 = bf16[2,192,1536]{2,1,0:T(8,128)(2,1)} custom-call(s32[2]{0:T(128)} %lens.1, bf16[2,192,1536]{2,1,0:T(8,128)(2,1)} %bitcast.6, f32[1536]{0:T(1024)} %gain_a.1, bf16[3,48,384]{2,1,0:T(8,128)(2,1)} %w_qkv.1, bf16[48,384]{1,0:T(8,128)(2,1)} %bitcast.7, f32[1536]{0:T(1024)} %gain_c.1, bf16[12,3072]{1,0:T(8,128)(2,1)} %w_pw1.1, bf16[12,1536]{1,0:T(8,128)(2,1)} %w_pw2.1, ...), custom_call_target="tpu_custom_call" | custom-call | tf_op jit(solution)/shard_map/layer/pallas_call | solution.py:430
  103.1 3.5 %copy.12 = bf16[192,2,1536]{2,1,0:T(2,128)(2,1)} copy(bf16[192,2,1536]{2,0,1:T(8,128)(2,1)} %bitcast.5) | data formatting | bytes 2359296 | tf_op jit(solution)/shard_map/transpose | solution.py:462

commit v4 on v3

--- a/solution.py
+++ b/solution.py
@@ -222,36 +222,42 @@
     assemble(0, 4, b1)
     W1.P1()
     O.R1()
+    QA.F()
+    QA.G()
     fn.wait_recv()
     fr.start()
     for copy in g2:
         copy.start()
-    QA.F()
-    O.P2()
-    W1.R1()
-    QB.S2()
-    QB.F()
-    QA.G()
-    for copy in (fm, fr):
-        copy.wait_recv()
-
-    def project(g):
+    fm.wait_recv()
+
+    def project(g, blocks):
         def step(m, carry):
             factor = jnp.where(m == 0, SCALE, 1.0).astype(F32)
             w = chunks(bq, slice(None), mat=(g, m))
-            v = jnp.dot(nrm[...].reshape(T, D), w, preferred_element_type=F32)
-            qkv[m, :, 384 * g : 384 * g + 384] = (v * factor).astype(BF)
+            for j in blocks:
+                rows = pl.ds(pl.multiple_of(j * L, 64), L)
+                v = jnp.dot(nrm[j], w, preferred_element_type=F32)
+                qkv[m, rows, 384 * g : 384 * g + 384] = (v * factor).astype(BF)
             return carry
 
         lax.fori_loop(0, 3, step, 0)
 
-    project(0)
+    project(0, (x, mate, near))
+    QB.S2()
+    QB.F()
+    W1.R1()
+    O.P2()
+    QB.G()
+    project(1, (x, mate, near))
+    O.R2()
+    W1.P2()
+    fr.wait_recv()
+    project(0, (far,))
+    project(1, (far,))
     for copy in g2:
         copy.wait_recv()
     assemble(4, 2, b2)
     W2.P1()
-    O.R2()
-    W1.P2()
 
     def send_pair(p, d):
         to = mod4(x + d)
@@ -292,26 +298,16 @@
         for d in (2, 1, 3):
             send_pair(p, d).start()
 
-        @pl.when(p == 0)
-        def _():
-            W2.R1()
-
-        @pl.when(p == 2)
-        def _():
-            O.S2()
-            O.F()
-
-        @pl.when(p == 3)
+        @pl.when(p == 4)
         def _():
             W1.R2()
-            W2.P2()
-
-        return carry
-
-    lax.fori_loop(0, 3, attend, 0)
-    QB.G()
-    project(1)
-    lax.fori_loop(3, 6, attend, 0)
+            O.S2()
+
+        return carry
+
+    lax.fori_loop(0, 6, attend, 0)
+    O.F()
+    W2.R1()
     for g in (0, 1):
         cols = pl.ds(pl.multiple_of(384 * mod4(x + 2 * g), 128), 384)
         ctx[a, :, cols] = ctxl[pl.ds(pl.multiple_of(x * L, L), L), 384 * g : 384 * g + 384]
@@ -340,9 +336,16 @@
 
     lax.fori_loop(0, 2 * (L // ROWS), norm_conv, 0)
     W1.S2()
+    W2.P2()
     W1.F()
     W1.G()
     time = x * L + lax.broadcasted_iota(jnp.int32, (L, 256), 0)
+
+    halo = []
+    for v in (0, 1):
+        at = lambda row: gp.at[:, pl.ds(row, EDGE), pl.ds(768 * v, 768)]
+        halo.append(rc("h+%d" % v, at(L), at(0), dp, mod4(x + 1)))
+        halo.append(rc("h-%d" % v, at(EDGE), at(EDGE + L), dp, mod4(x + 3)))
 
     def glu(n, carry):
         lanes = pl.ds(pl.multiple_of(n * 256, 256), 256)
@@ -357,23 +360,26 @@
 
         @pl.when(n == 2)
         def _():
+            halo[0].start()
+            halo[1].start()
+
+        @pl.when(n == 4)
+        def _():
             W2.R2()
 
         return carry
 
     lax.fori_loop(0, 6, glu, 0)
-    hp = rc("h+", gp.at[:, pl.ds(L, EDGE)], gp.at[:, pl.ds(0, EDGE)], dp, mod4(x + 1))
-    hm = rc("h-", gp.at[:, pl.ds(EDGE, EDGE)], gp.at[:, pl.ds(EDGE + L, EDGE)], dp, mod4(x + 3))
-    hp.start()
-    hm.start()
+    halo[2].start()
+    halo[3].start()
     W2.S2()
-    hp.wait_recv()
-    hm.wait_recv()
+    halo[0].wait_recv()
+    halo[1].wait_recv()
     first = jnp.where(x == 0, 0.0, 1.0).astype(F32)
     last = jnp.where(x == 3, 0.0, 1.0).astype(F32)
 
     def conv(i, carry):
-        u, n = lax.div(i, 12), lax.rem(i, 12)
+        u, n = lax.rem(i, 2), lax.div(i, 2)
         lanes = pl.ds(pl.multiple_of(n * 128, 128), 128)
         cf[0:EDGE, :] = gp[u, 0:EDGE, lanes].astype(F32) * first
         cf[EDGE : EDGE + L, :] = gp[u, EDGE : EDGE + L, lanes].astype(F32)
@@ -385,7 +391,10 @@
         dep[u, :, lanes] = total
         return carry
 
-    lax.fori_loop(0, 24, conv, 0)
+    lax.fori_loop(0, 12, conv, 0)
+    halo[2].wait_recv()
+    halo[3].wait_recv()
+    lax.fori_loop(12, 24, conv, 0)
     W2.F()
 
     def norm_mid(i, carry):
@@ -411,7 +420,7 @@
 
     for ring in (QA, QB, O, W1, W2):
         ring.done()
-    for copy in [qx] + ox + g1 + g2 + [fn, fm, fr, hp, hm]:
+    for copy in [qx] + ox + g1 + g2 + [fn, fm, fr] + halo:
         copy.wait_send()
 
     def leave(p, carry):

time: 107 us -> 101 us (0.944)
  Pallas kernels: 101 us -> 94.9 us
    pallas_call x1, Pallas kernels: 101 us -> 94.9 us  [local(): pl.pallas_call(body, out_shape=jax.ShapeDtypeStruct((2, L, D), BF), in_sp...]
where the time goes in v4:
time: 101 us
  Pallas kernels  94.9 us (94%)
  local copies, waits for them, and re-layouts  5.9 us (6%)
    pallas_call x1, Pallas kernels, local(): pl.pallas_call(body, out_shape=jax.ShapeDtypeStruct((2, L, D), BF), in_sp...  94.9 us
    transpose x1, local copies, waits for them, and re-layouts, local(): return jnp.swapaxes(result, 0, 1)  3.5 us
    unnamed x1, local copies, waits for them, and re-layouts  2.4 us

profile of v4, /device:TPU:1, one launch (start us, length us, event | category | flops | bytes accessed | tf_op | source)
XLA Modules:
  0.0 100.9 jit_solution(7294455565429889134)
XLA Ops:
  0.0 2.4 %copy.14 = bf16[192,2,1536]{2,0,1:T(8,128)(2,1)} copy(bf16[192,2,1536]{2,1,0:T(2,128)(2,1)} %param.10) | data formatting | bytes 2359296 | tf_op args[0]
  2.4 94.9 %layer.1 = bf16[2,192,1536]{2,1,0:T(8,128)(2,1)} custom-call(s32[2]{0:T(128)} %lens.1, bf16[2,192,1536]{2,1,0:T(8,128)(2,1)} %bitcast.6, f32[1536]{0:T(1024)} %gain_a.1, bf16[3,48,384]{2,1,0:T(8,128)(2,1)} %w_qkv.1, bf16[48,384]{1,0:T(8,128)(2,1)} %bitcast.7, f32[1536]{0:T(1024)} %gain_c.1, bf16[12,3072]{1,0:T(8,128)(2,1)} %w_pw1.1, bf16[12,1536]{1,0:T(8,128)(2,1)} %w_pw2.1, ...), custom_call_target="tpu_custom_call" | custom-call | tf_op jit(solution)/shard_map/layer/pallas_call | solution.py:439
  97.4 3.5 %copy.12 = bf16[192,2,1536]{2,1,0:T(2,128)(2,1)} copy(bf16[192,2,1536]{2,0,1:T(8,128)(2,1)} %bitcast.5) | data formatting | bytes 2359296 | tf_op jit(solution)/shard_map/transpose | solution.py:471

commit v5 on v4

--- a/solution.py
+++ b/solution.py
@@ -44,8 +44,8 @@
 
 
 def body(
-    lens, frames, gain_a, w_qkv, w_out, gain_c, w_pw1, w_pw2, taps, gain_m, out,
-    bq, bo, b1, b2, xg, nrm, nsend, qkv, kbias, ctxl, ctx, res, cin, gp, cf, dep, send, recv,
+    lens, raw, gain_a, w_qkv, w_out, gain_c, w_pw1, w_pw2, taps, gain_m, out,
+    bq, bo, b1, b2, xg, nrm, nsend, qkv, kbias, ctxl, ctx, res, cin, gp, cf, dep, frames, send, recv,
 ):
     x = lax.axis_index("seq")
     dp = lax.axis_index("dp")
@@ -172,10 +172,19 @@
     xg[x] = jnp.zeros((16, 3 * D), BF)
     xg[x, 0:12, 0 : 2 * D] = w_pw1[...]
     xg[x, 0:12, 2 * D :] = w_pw2[...]
+
+    def split(i, carry):
+        rows = pl.ds(pl.multiple_of(i * 48, 16), 48)
+        v = raw[rows].astype(F32)
+        for u in (0, 1):
+            frames[u, rows, :] = v[:, u, :].astype(BF)
+        return carry
+
+    lax.fori_loop(0, L // 48, split, 0)
     pl.semaphore_wait(barrier, len(peers))
     qx.start()
     QA.P1()
-    for copy in ox + g1:
+    for copy in ox + g1 + g2:
         copy.start()
 
     def normed(u, target):
@@ -205,7 +214,7 @@
     O.P1()
     QA.S2()
     QB.R2()
-    for copy in g1:
+    for copy in g1 + g2:
         copy.wait_recv()
 
     r = lax.broadcasted_iota(jnp.int32, (48, 64), 0)
@@ -220,14 +229,14 @@
             target[c, B, A, :, 768 * n : 768 * n + 768] = rows
 
     assemble(0, 4, b1)
+    assemble(4, 2, b2)
     W1.P1()
+    W2.P1()
     O.R1()
     QA.F()
     QA.G()
     fn.wait_recv()
     fr.start()
-    for copy in g2:
-        copy.start()
     fm.wait_recv()
 
     def project(g, blocks):
@@ -246,6 +255,7 @@
     QB.S2()
     QB.F()
     W1.R1()
+    W2.R1()
     O.P2()
     QB.G()
     project(1, (x, mate, near))
@@ -254,10 +264,6 @@
     fr.wait_recv()
     project(0, (far,))
     project(1, (far,))
-    for copy in g2:
-        copy.wait_recv()
-    assemble(4, 2, b2)
-    W2.P1()
 
     def send_pair(p, d):
         to = mod4(x + d)
@@ -301,13 +307,13 @@
         @pl.when(p == 4)
         def _():
             W1.R2()
+            W2.P2()
             O.S2()
 
         return carry
 
     lax.fori_loop(0, 6, attend, 0)
     O.F()
-    W2.R1()
     for g in (0, 1):
         cols = pl.ds(pl.multiple_of(384 * mod4(x + 2 * g), 128), 384)
         ctx[a, :, cols] = ctxl[pl.ds(pl.multiple_of(x * L, L), L), 384 * g : 384 * g + 384]
@@ -336,7 +342,6 @@
 
     lax.fori_loop(0, 2 * (L // ROWS), norm_conv, 0)
     W1.S2()
-    W2.P2()
     W1.F()
     W1.G()
     time = x * L + lax.broadcasted_iota(jnp.int32, (L, 256), 0)
@@ -363,7 +368,7 @@
             halo[0].start()
             halo[1].start()
 
-        @pl.when(n == 4)
+        @pl.when(n == 0)
         def _():
             W2.R2()
 
@@ -434,7 +439,6 @@
 def local(
     frames, lengths, attn_gain, w_qkv, w_out, conv_gain, w_pw1, depth_kernel, mid_gain, w_pw2
 ):
-    rows = jnp.swapaxes(frames, 0, 1)
     vmem = pl.BlockSpec(memory_space=pltpu.VMEM)
     result = pl.pallas_call(
         body,
@@ -458,6 +462,7 @@
             pltpu.VMEM((2, L + 2 * EDGE, D), BF),
             pltpu.VMEM((L + 2 * EDGE, 128), F32),
             pltpu.VMEM((2, L, D), F32),
+            pltpu.VMEM((2, L, D), BF),
             pltpu.SemaphoreType.DMA((NSEM,)),
             pltpu.SemaphoreType.DMA((NSEM,)),
         ],
@@ -466,7 +471,7 @@
         ),
         name="layer",
     )(
-        lengths, rows, attn_gain, w_qkv, w_out.T, conv_gain, w_pw1, w_pw2, depth_kernel, mid_gain,
+        lengths, frames, attn_gain, w_qkv, w_out.T, conv_gain, w_pw1, w_pw2, depth_kernel, mid_gain,
     )
     return jnp.swapaxes(result, 0, 1)
 

time: 101 us -> 99.1 us (0.981)
  local copies, waits for them, and re-layouts: 5.9 us -> 3.5 us
    unnamed x1 -> x0, local copies, waits for them, and re-layouts: 2.4 us -> none
where the time goes in v5:
time: 99.1 us; the launch traced here: 99 us
  Pallas kernels  95.5 us (96%)
  local copies, waits for them, and re-layouts  3.5 us (4%)
    pallas_call x1, Pallas kernels, local(): pl.pallas_call(body, out_shape=jax.ShapeDtypeStruct((2, L, D), BF), in_sp...  95.5 us
    transpose x1, local copies, waits for them, and re-layouts, local(): return jnp.swapaxes(result, 0, 1)  3.5 us

profile of v5, /device:TPU:1, one launch (start us, length us, event | category | flops | bytes accessed | tf_op | source)
XLA Modules:
  0.0 99.0 jit_solution(7192377428855242589)
XLA Ops:
  0.0 95.5 %layer.1 = bf16[2,192,1536]{2,1,0:T(8,128)(2,1)} custom-call(s32[2]{0:T(128)} %lens.1, bf16[192,2,1536]{2,1,0:T(2,128)(2,1)} %raw.1, f32[1536]{0:T(1024)} %gain_a.1, bf16[3,48,384]{2,1,0:T(8,128)(2,1)} %w_qkv.1, bf16[48,384]{1,0:T(8,128)(2,1)} %bitcast.3, f32[1536]{0:T(1024)} %gain_c.1, bf16[12,3072]{1,0:T(8,128)(2,1)} %w_pw1.1, bf16[12,1536]{1,0:T(8,128)(2,1)} %w_pw2.1, ...), custom_call_target="tpu_custom_call" | custom-call | tf_op jit(solution)/shard_map/layer/pallas_call | solution.py:443
  95.5 3.5 %copy.11 = bf16[192,2,1536]{2,1,0:T(2,128)(2,1)} copy(bf16[192,2,1536]{2,0,1:T(8,128)(2,1)} %bitcast.2) | data formatting | bytes 2359296 | tf_op jit(solution)/shard_map/transpose | solution.py:476

commit v6 on v5

--- a/solution.py
+++ b/solution.py
@@ -173,6 +173,12 @@
     xg[x, 0:12, 0 : 2 * D] = w_pw1[...]
     xg[x, 0:12, 2 * D :] = w_pw2[...]
 
+    pl.semaphore_wait(barrier, len(peers))
+    qx.start()
+    QA.P1()
+    for copy in ox + g1 + g2:
+        copy.start()
+
     def split(i, carry):
         rows = pl.ds(pl.multiple_of(i * 48, 16), 48)
         v = raw[rows].astype(F32)
@@ -181,11 +187,6 @@
         return carry
 
     lax.fori_loop(0, L // 48, split, 0)
-    pl.semaphore_wait(barrier, len(peers))
-    qx.start()
-    QA.P1()
-    for copy in ox + g1 + g2:
-        copy.start()
 
     def normed(u, target):
         def step(i, carry):
@@ -374,7 +375,7 @@
 
         return carry
 
-    lax.fori_loop(0, 6, glu, 0)
+    lax.fori_loop(0, 6, glu, 0, unroll=2)
     halo[2].start()
     halo[3].start()
     W2.S2()
@@ -396,10 +397,10 @@
         dep[u, :, lanes] = total
         return carry
 
-    lax.fori_loop(0, 12, conv, 0)
+    lax.fori_loop(0, 12, conv, 0, unroll=2)
     halo[2].wait_recv()
     halo[3].wait_recv()
-    lax.fori_loop(12, 24, conv, 0)
+    lax.fori_loop(12, 24, conv, 0, unroll=2)
     W2.F()
 
     def norm_mid(i, carry):
@@ -421,7 +422,7 @@
             out[u, :, lanes] = jnp.where(time < lens[u], total, 0.0).astype(BF)
         return carry
 
-    lax.fori_loop(0, 6, last_product, 0)
+    lax.fori_loop(0, 6, last_product, 0, unroll=2)
 
     for ring in (QA, QB, O, W1, W2):
         ring.done()

time: 99.1 us -> 97.6 us (0.985)
  Pallas kernels: 95.5 us -> 93.9 us
    pallas_call x1, Pallas kernels: 95.5 us -> 93.9 us  [local(): pl.pallas_call(body, out_shape=jax.ShapeDtypeStruct((2, L, D), BF), in_sp...]
where the time goes in v6:
time: 97.6 us; the launch traced here: 97.4 us
  Pallas kernels  93.9 us (96%)
  local copies, waits for them, and re-layouts  3.5 us (4%)
    pallas_call x1, Pallas kernels, local(): pl.pallas_call(body, out_shape=jax.ShapeDtypeStruct((2, L, D), BF), in_sp...  93.9 us
    transpose x1, local copies, waits for them, and re-layouts, local(): return jnp.swapaxes(result, 0, 1)  3.5 us

profile of v6, /device:TPU:1, one launch (start us, length us, event | category | flops | bytes accessed | tf_op | source)
XLA Modules:
  0.0 97.4 jit_solution(15741499342454888742)
XLA Ops:
  0.0 93.9 %layer.1 = bf16[2,192,1536]{2,1,0:T(8,128)(2,1)} custom-call(s32[2]{0:T(128)} %lens.1, bf16[192,2,1536]{2,1,0:T(2,128)(2,1)} %raw.1, f32[1536]{0:T(1024)} %gain_a.1, bf16[3,48,384]{2,1,0:T(8,128)(2,1)} %w_qkv.1, bf16[48,384]{1,0:T(8,128)(2,1)} %bitcast.3, f32[1536]{0:T(1024)} %gain_c.1, bf16[12,3072]{1,0:T(8,128)(2,1)} %w_pw1.1, bf16[12,1536]{1,0:T(8,128)(2,1)} %w_pw2.1, ...), custom_call_target="tpu_custom_call" | custom-call | tf_op jit(solution)/shard_map/layer/pallas_call | solution.py:444
  93.9 3.5 %copy.11 = bf16[192,2,1536]{2,1,0:T(2,128)(2,1)} copy(bf16[192,2,1536]{2,0,1:T(8,128)(2,1)} %bitcast.2) | data formatting | bytes 2359296 | tf_op jit(solution)/shard_map/transpose | solution.py:477

commit v7 on v6

--- a/solution.py
+++ b/solution.py
@@ -313,7 +313,7 @@
 
         return carry
 
-    lax.fori_loop(0, 6, attend, 0)
+    lax.fori_loop(0, 6, attend, 0, unroll=2)
     O.F()
     for g in (0, 1):
         cols = pl.ds(pl.multiple_of(384 * mod4(x + 2 * g), 128), 384)

time: 97.6 us -> 97.7 us (level)
  no operation moved by 1% of the time
where the time goes in v7:
time: 97.7 us; the launch traced here: 97.6 us
  Pallas kernels  94.1 us (96%)
  local copies, waits for them, and re-layouts  3.5 us (4%)
    pallas_call x1, Pallas kernels, local(): pl.pallas_call(body, out_shape=jax.ShapeDtypeStruct((2, L, D), BF), in_sp...  94.1 us
    transpose x1, local copies, waits for them, and re-layouts, local(): return jnp.swapaxes(result, 0, 1)  3.5 us

profile of v7, /device:TPU:1, one launch (start us, length us, event | category | flops | bytes accessed | tf_op | source)
XLA Modules:
  0.0 97.6 jit_solution(7524866021161757927)
XLA Ops:
  0.0 94.1 %layer.1 = bf16[2,192,1536]{2,1,0:T(8,128)(2,1)} custom-call(s32[2]{0:T(128)} %lens.1, bf16[192,2,1536]{2,1,0:T(2,128)(2,1)} %raw.1, f32[1536]{0:T(1024)} %gain_a.1, bf16[3,48,384]{2,1,0:T(8,128)(2,1)} %w_qkv.1, bf16[48,384]{1,0:T(8,128)(2,1)} %bitcast.3, f32[1536]{0:T(1024)} %gain_c.1, bf16[12,3072]{1,0:T(8,128)(2,1)} %w_pw1.1, bf16[12,1536]{1,0:T(8,128)(2,1)} %w_pw2.1, ...), custom_call_target="tpu_custom_call" | custom-call | tf_op jit(solution)/shard_map/layer/pallas_call | solution.py:444
  94.1 3.5 %copy.11 = bf16[192,2,1536]{2,1,0:T(2,128)(2,1)} copy(bf16[192,2,1536]{2,0,1:T(8,128)(2,1)} %bitcast.2) | data formatting | bytes 2359296 | tf_op jit(solution)/shard_map/transpose | solution.py:477
